TPU v7x, 32 devices: a whole 2x2x4 slice. The times are simulated.
32 devices in a mesh: space: 8 (over z, x), tm: 4 (over y, core).
Axes of the slice: x: 2, y: 2, z: 4, core: 2. Of those that a mesh axis runs over, the one named last changes fastest.
Arguments:
- snapshots: float32 [4608, 8192], P('tm', 'space'), as said below
- block_starts: int32 [32], P('tm'), may hold values from 0 to 4352, as said below
- owner: int32 [9], replicated, may hold values from 0 to 3, as said below
Outputs:
- modes: float32 [20, 32, 2, 8192], P('tm', None, None, 'space')
Inputs may be any that keep to these rules, and one draw needn't show every extreme that they name: `block_starts`: block k lies inside the snapshots held by index k // 8 of tm: its start is that range's first snapshot plus an even offset of 0 to 896; within one range the starts rise with k by 112 or more, the range's first block starts at offset 0 and its last at 896. `owner`: one index of tm owns exactly 5 frequencies, every other index owns one or more and fewer than 5. `snapshots`: finite real values.
All inputs are finite; a program needn't handle non-finite values.
Results may differ from a plain program's by a relative error of at most 0.0003.
Values sent between devices are 32-bit elements; how exact they have to be, the bound alone decides.
A program may use at most 64 MiB of HBM per device.

v0:
```python
import jax
import jax.numpy as jnp
from jax import lax
from jax.sharding import PartitionSpec as P

NFFT = 256
NF = 9
FCAP = 5


def dft_table():
    times = jnp.arange(NFFT, dtype=jnp.int32)
    freqs = jnp.arange(NF, dtype=jnp.int32)
    phase = freqs[:, None] * times[None, :] % NFFT
    angle = 2.0 * jnp.pi / NFFT * phase.astype(jnp.float32)
    window = 0.5 - 0.5 * jnp.cos(2.0 * jnp.pi / NFFT * times.astype(jnp.float32))
    return jnp.stack([window * jnp.cos(angle), -window * jnp.sin(angle)], axis=1)


def slot_selector(owner, slot_count):
    freq_ids = jnp.arange(owner.shape[0], dtype=jnp.int32)
    before = (owner[None, :] == owner[:, None]) & (freq_ids[None, :] < freq_ids[:, None])
    rank_in = jnp.sum(before.astype(jnp.int32), axis=1)
    slot_of = owner * FCAP + rank_in
    targets = jnp.arange(slot_count, dtype=jnp.int32)
    return (slot_of[None, :] == targets[:, None]).astype(jnp.float32)


def partial_gram(matrices):
    return jnp.einsum("kip,kjp->kij", matrices, matrices, precision=lax.Precision.HIGHEST)


def finish_pass(matrices, totals, rows_total):
    gram = totals / rows_total
    identity = jnp.eye(gram.shape[-1], dtype=jnp.float32)
    diagonal_sum = jnp.trace(gram, axis1=1, axis2=2)
    gram = gram + jnp.where(diagonal_sum == 0.0, 1.0, 0.0)[:, None, None] * identity
    factor = jnp.linalg.cholesky(gram)
    inverse = jax.scipy.linalg.solve_triangular(
        factor, jnp.broadcast_to(identity, gram.shape), lower=True
    )
    return jnp.einsum("kij,kjp->kip", inverse, matrices, precision=lax.Precision.HIGHEST)


def local(snapshots, block_starts, owner):
    table = dft_table()
    samples, points = snapshots.shape
    block_count = block_starts.shape[0]
    tm_count = lax.axis_size("tm")
    space_count = lax.axis_size("space")
    rows_total = 2.0 * points * space_count
    column_count = block_count * tm_count
    offset = lax.axis_index("tm") * samples
    segments = jnp.stack(
        [
            lax.dynamic_slice_in_dim(snapshots, block_starts[block] - offset, NFFT, 0)
            for block in range(block_count)
        ]
    )
    spectra = jnp.einsum("fct,btp->fbcp", table, segments, precision=lax.Precision.HIGHEST)
    selector = slot_selector(owner, tm_count * FCAP)
    outgoing = jnp.einsum("lf,fbcp->lbcp", selector, spectra, precision=lax.Precision.HIGHEST)
    outgoing = outgoing.reshape(tm_count, FCAP, block_count, 2, points)
    received = lax.all_to_all(outgoing, "tm", split_axis=0, concat_axis=2, tiled=True)
    count = received.shape[1]
    matrices = received[0].reshape(count, column_count, 2 * points)
    for turn in range(2):
        partial_sums = partial_gram(matrices)
        totals = lax.psum(partial_sums, "space")
        matrices = finish_pass(matrices, totals, rows_total)
    return matrices.reshape(count, column_count, 2, points)


def solution(mesh):
    placed = (P("tm", "space"), P("tm"), P())
    return jax.shard_map(
        local, mesh=mesh, in_specs=placed, out_specs=P("tm", None, None, "space"), check_vma=False
    )
```

profile of v0, /device:TPU:0, one launch (start us, length us, event | category | flops | bytes accessed | tf_op | source)
XLA Modules:
  0.0 195.6 jit_solution(8554536515295902344)
XLA Ops:
  0.0 1.6 fusion.29
  6.7 0.9 convert_reduce_fusion
  7.6 0.7 multiply_add_fusion.2
  8.3 2.4 %bitcast_dynamic-update-slice_fusion.7 = f32[8,256,1024]{2,1,0:T(8,128)} fusion(f32[1152,1024]{1,0:T(8,128)} %param.6, s32[]{:T(128)S(6)} %select_n.70), kind=kLoop, calls=%fused_computation.10 | loop fusion | bytes 2097156
  10.7 2.4 %bitcast_dynamic-update-slice_fusion.6 = f32[8,256,1024]{2,1,0:T(8,128)} fusion(f32[8,256,1024]{2,1,0:T(8,128)} %bitcast_dynamic-update-slice_fusion.7, f32[1152,1024]{1,0:T(8,128)} %param.6, s32[]{:T(128)S(6)} %select_n.71), kind=kLoop, calls=%fused_computation.9 | loop fusion | bytes 2097156
  13.1 2.4 %bitcast_dynamic-update-slice_fusion.5 = f32[8,256,1024]{2,1,0:T(8,128)} fusion(f32[8,256,1024]{2,1,0:T(8,128)} %bitcast_dynamic-update-slice_fusion.6, f32[1152,1024]{1,0:T(8,128)} %param.6, s32[]{:T(128)S(6)} %select_n.72), kind=kLoop, calls=%fused_computation.8 | loop fusion | bytes 2097156
  15.5 2.4 %bitcast_dynamic-update-slice_fusion.4 = f32[8,256,1024]{2,1,0:T(8,128)} fusion(f32[8,256,1024]{2,1,0:T(8,128)} %bitcast_dynamic-update-slice_fusion.5, f32[1152,1024]{1,0:T(8,128)} %param.6, s32[]{:T(128)S(6)} %select_n.73), kind=kLoop, calls=%fused_computation.7 | loop fusion | bytes 2097156
  17.9 2.4 %bitcast_dynamic-update-slice_fusion.3 = f32[8,256,1024]{2,1,0:T(8,128)} fusion(f32[8,256,1024]{2,1,0:T(8,128)} %bitcast_dynamic-update-slice_fusion.4, f32[1152,1024]{1,0:T(8,128)} %param.6, s32[]{:T(128)S(6)} %select_n.74), kind=kLoop, calls=%fused_computation.6 | loop fusion | bytes 2097156
  20.2 2.4 %bitcast_dynamic-update-slice_fusion.2 = f32[8,256,1024]{2,1,0:T(8,128)} fusion(f32[8,256,1024]{2,1,0:T(8,128)} %bitcast_dynamic-update-slice_fusion.3, f32[1152,1024]{1,0:T(8,128)} %param.6, s32[]{:T(128)S(6)} %select_n.75), kind=kLoop, calls=%fused_computation.5 | loop fusion | bytes 2097156
  22.7 2.4 %bitcast_dynamic-update-slice_fusion.1 = f32[8,256,1024]{2,1,0:T(8,128)} fusion(f32[8,256,1024]{2,1,0:T(8,128)} %bitcast_dynamic-update-slice_fusion.2, f32[1152,1024]{1,0:T(8,128)} %param.6, s32[]{:T(128)S(6)} %select_n.76), kind=kLoop, calls=%fused_computation.4 | loop fusion | bytes 2097156
  25.1 2.4 %bitcast_dynamic-update-slice_fusion = f32[8,256,1024]{2,1,0:T(8,128)} fusion(f32[8,256,1024]{2,1,0:T(8,128)} %bitcast_dynamic-update-slice_fusion.1, f32[1152,1024]{1,0:T(8,128)} %param.6, s32[]{:T(128)S(6)} %select_n.77), kind=kLoop, calls=%fused_computation.3 | loop fusion | bytes 2097156 | tf_op jit(solution)/shard_map/stack | solution.py:54
  27.4 0.1 sine_multiply_fusion
  27.5 7.5 %fusion.2 = f32[9,8,2,1024]{3,0,2,1:T(8,128)S(1)} fusion(f32[8,256,1024]{2,1,0:T(8,128)} %bitcast_dynamic-update-slice_fusion, f32[9,1,256]{2,0,1:T(8,128)S(1)} %get-tuple-element.15, f32[9,1,256]{2,0,1:T(8,128)S(1)} %get-tuple-element.16), kind=kOutput, calls=%fused_computation.2 | convolution fusion | flops 452989440 | bytes 8996864 | tf_op jit(solution)/shard_map/fct,btp->fbcp/dot_general | solution.py:60
  35.0 0.9 fusion.23
  35.9 1.8 copy.15
  37.7 4.2 %all-to-all-start = ((f32[4,5,8,2,1024]{4,2,3,1,0:T(8,128)}), f32[4,5,8,2,1024]{4,2,3,1,0:T(8,128)S(1)}, u32[]{:S(2)}, u32[]{:S(2)}) async-start(f32[4,5,8,2,1024]{4,2,3,1,0:T(8,128)} %bitcast.22), calls=%async_computation | async-start | bytes 2621440 | tf_op jit(solution)/shard_map/all_to_all | solution.py:64
  42.0 17.2 %all-to-all-done = f32[4,5,8,2,1024]{4,2,3,1,0:T(8,128)S(1)} async-done(((f32[4,5,8,2,1024]{4,2,3,1,0:T(8,128)}), f32[4,5,8,2,1024]{4,2,3,1,0:T(8,128)S(1)}, u32[]{:S(2)}, u32[]{:S(2)}) %all-to-all-start) | async-done | bytes 1310752 | tf_op jit(solution)/shard_map/all_to_all | solution.py:64
  59.2 0.1 copy.16
  59.4 1.2 fusion.30
  60.6 39.1 %psum.14 = f32[5,32,32]{1,2,0:T(8,128)S(1)} all-reduce(f32[5,32,32]{1,2,0:T(8,128)S(1)} %fusion.30), channel_id=1, replica_groups=mesh['space'=8,'tm'=4] {'space'}, use_global_device_ids=true, to_apply=%region_1.2 | all-reduce | flops 5120 | bytes 40960 | tf_op jit(solution)/shard_map/psum | solution.py:69
  99.8 0.1 select_reduce_fusion.3
  99.9 0.1 multiply_add_fusion.1
  100.0 0.1 copy.18
  100.1 0.1 fusion.10
  100.2 14.7 %custom-call.8 = f32[5,32,32]{2,1,0:T(8,128)S(1)} custom-call(f32[5,32,32]{2,1,0:T(8,128)S(1)} %fusion.10), custom_call_target="Cholesky" | custom-call | tf_op jit(solution)/shard_map/jit(cholesky)/cholesky | solution.py:38
  114.9 0.1 compare_reduce_fusion.1
  115.0 0.1 select_bitcast_fusion.1
  115.1 12.3 %custom-call.9 = f32[5,1,32,32]{2,3,1,0:T(8,128)S(1)} custom-call(f32[5,1,32,32]{3,2,1,0:T(8,128)S(1)} %select_bitcast_fusion.1), custom_call_target="InvertDiagBlocksLowerTriangular" | custom-call | tf_op jit(solution)/shard_map/jit(_solve_triangular)/vmap()/triangular_solve | solution.py:39
  127.4 0.3 fusion.8
  127.7 1.2 fusion.31
  129.0 1.2 fusion.32
  130.2 34.0 %psum.15 = f32[5,32,32]{1,2,0:T(8,128)S(1)} all-reduce(f32[5,32,32]{1,2,0:T(8,128)S(1)} %fusion.32), channel_id=1, replica_groups=mesh['space'=8,'tm'=4] {'space'}, use_global_device_ids=true, to_apply=%region_5.8 | all-reduce | flops 5120 | bytes 40960 | tf_op jit(solution)/shard_map/psum | solution.py:69
  164.3 0.1 select_reduce_fusion.2
  164.4 0.1 multiply_add_fusion
  164.5 0.1 copy.22
  164.6 0.1 fusion.7
  164.7 14.7 %custom-call.10 = f32[5,32,32]{2,1,0:T(8,128)S(1)} custom-call(f32[5,32,32]{2,1,0:T(8,128)S(1)} %fusion.7), custom_call_target="Cholesky" | custom-call | tf_op jit(solution)/shard_map/jit(cholesky)/cholesky | solution.py:38
  179.3 0.1 compare_reduce_fusion
  179.5 0.1 select_bitcast_fusion
  179.6 12.3 %custom-call.11 = f32[5,1,32,32]{2,3,1,0:T(8,128)S(1)} custom-call(f32[5,1,32,32]{3,2,1,0:T(8,128)S(1)} %select_bitcast_fusion), custom_call_target="InvertDiagBlocksLowerTriangular" | custom-call | tf_op jit(solution)/shard_map/jit(_solve_triangular)/vmap()/triangular_solve | solution.py:39
  191.9 0.3 fusion.5
  192.2 1.2 fusion.33
  193.4 2.2 %reshape.155 = f32[5,32,2,1024]{3,2,1,0:T(2,128)} reshape(f32[5,32,2048]{2,1,0:T(8,128)S(1)} %fusion.33) | data formatting | bytes 2621440 | tf_op jit(solution)/shard_map/reshape | solution.py:71
  (10 shorter events, 0.2 us)
Async XLA Ops:
  37.7 21.5 %all-to-all-start = ((f32[4,5,8,2,1024]{4,2,3,1,0:T(8,128)}), f32[4,5,8,2,1024]{4,2,3,1,0:T(8,128)S(1)}, u32[]{:S(2)}, u32[]{:S(2)}) async-start(f32[4,5,8,2,1024]{4,2,3,1,0:T(8,128)} %bitcast.22), calls=%async_computation | async-start | bytes 2621440 | tf_op jit(solution)/shard_map/all_to_all | solution.py:64
where the time goes:
time: 196 us
  blocking collectives  73.2 us (37%)
  other arithmetic  56.8 us (29%)
  local copies, waits for them, and re-layouts  25.1 us (13%)
  waiting for transfers between devices  17.2 us (9%)
  matrix products  14 us (7%)
  between operations  5.13 us (3%)
  starting transfers between devices  4.24 us (2%)
    psum x2, blocking collectives, local(): totals = lax.psum(partial_sums, 'space')  73.2 us
    another operation x7, other arithmetic, finish_pass(): factor = jnp.linalg.cholesky(gram)  29.6 us
    another operation x5, other arithmetic, finish_pass(): jax.scipy.linalg.solve_triangular(factor, jnp.broadcast_to(identity, gram...  24.8 us
    all_to_all x1, waiting for transfers between devices, local(): lax.all_to_all(outgoing, 'tm', split_axis=0, concat_axis=2, tiled=True)  17.2 us
    unnamed x7, local copies, waits for them, and re-layouts  16.8 us
    dot_general x1, matrix products, local(): jnp.einsum('fct,btp->fbcp', table, segments, precision=lax.Precision.HIGH...  7.49 us
    all_to_all x1, starting transfers between devices, local(): lax.all_to_all(outgoing, 'tm', split_axis=0, concat_axis=2, tiled=True)  4.24 us
  transfers between devices with their start and end apart: 1, of which 1 were waited for; matrix products, arithmetic and copies ran while one was open for 0% of the time, Pallas kernels for 0%

commit v1 on v0

v1 whole, which is shorter than its diff:
```python
import functools

import jax
import jax.numpy as jnp
import numpy as np
from jax import lax
from jax.experimental import pallas as pl
from jax.experimental.pallas import tpu as pltpu
from jax.sharding import PartitionSpec as P

NFFT = 256
NF = 9
FCAP = 5
ROWS = 2 * NF
QP = 256
F32 = jnp.float32
BF16 = jnp.bfloat16
MESH = pl.DeviceIdType.MESH


def dft_table():
    times = np.arange(NFFT)
    phase = (np.arange(NF)[:, None] * times[None, :]) % NFFT
    angle = 2.0 * np.pi / NFFT * phase
    window = 0.5 - 0.5 * np.cos(2.0 * np.pi / NFFT * times)
    table = np.stack([window * np.cos(angle), -window * np.sin(angle)], axis=1)
    return table.reshape(ROWS, NFFT).astype(np.float32)


def split3(x):
    a = x.astype(BF16)
    rest = x - a.astype(F32)
    b = rest.astype(BF16)
    c = (rest - b.astype(F32)).astype(BF16)
    return a, b, c


def split2(x):
    a = x.astype(BF16)
    return a, (x - a.astype(F32)).astype(BF16)


def mm(a, b):
    return jnp.dot(a, b, preferred_element_type=F32)


def mm_t(a, b):
    return lax.dot_general(a, b, (((1,), (1,)), ((), ())), preferred_element_type=F32)


def pack(square):
    n = square.shape[0] // 4
    return jnp.concatenate([square[n * i : n * i + n] for i in range(4)], axis=1)


def unpack(packed):
    n = packed.shape[1] // 4
    return jnp.concatenate([packed[:, n * i : n * i + n] for i in range(4)], axis=0)


def inverse_factor(gram, panel=8):
    n = gram.shape[0]
    row = lax.broadcasted_iota(jnp.int32, (n, n), 0)
    col = lax.broadcasted_iota(jnp.int32, (n, n), 1)
    eye = jnp.where(row == col, 1.0, 0.0).astype(F32)
    trace = jnp.sum(jnp.sum(gram * eye, axis=1, keepdims=True), axis=0, keepdims=True)
    gram = gram + jnp.where(trace == 0.0, 1.0, 0.0) * eye
    work = jnp.concatenate([eye, gram, jnp.zeros((n, 128 - 2 * n), F32)], axis=1)
    rows = lax.broadcasted_iota(jnp.int32, (n, 128), 0)
    diag = jnp.ones((n, 128), F32)
    for first in range(0, n, panel):
        cols = [
            jnp.broadcast_to(work[:, n + first + j : n + first + j + 1], (n, 128))
            for j in range(panel)
        ]
        for j in range(panel):
            k = first + j
            pivot = jnp.broadcast_to(cols[j][k : k + 1], (n, 128))
            diag = jnp.where(rows == k, pivot, diag)
            factor = jnp.where(rows > k, cols[j] / pivot, 0.0)
            work = work - factor * work[k : k + 1]
            for i in range(j + 1, panel):
                cols[i] = cols[i] - factor * cols[i][k : k + 1]
    return (work / jnp.sqrt(diag))[:, :n]


def kernel(
    tms, sps, starts_ref, owner_ref, tab_ref, snap_hbm, out_ref,
    snap, tallf, tall, spec, send, recv, xs, bs, gacc, packed, gbuf, pinv, ibuf, bd,
    snap_sem, a2a_send, a2a_recv, g_send, g_recv, i_send, i_recv,
):
    quarters, samples = snap.shape[0], snap.shape[1]
    blocks = starts_ref.shape[0]
    nb = blocks * tms
    rows_total = 2.0 * quarters * QP * sps
    me = lax.axis_index("tm")
    my = lax.axis_index("space")
    first_worker = sps // 4

    loads = [
        pltpu.make_async_copy(snap_hbm.at[:, pl.ds(q * QP, QP)], snap.at[q], snap_sem.at[q])
        for q in range(quarters)
    ]
    for load in loads:
        load.start()
    barrier = pltpu.get_barrier_semaphore()
    for r in range(1, tms):
        pl.semaphore_signal(barrier, inc=1, device_id={"tm": lax.rem(me + r, tms)}, device_id_type=MESH)
    for r in range(1, sps):
        pl.semaphore_signal(barrier, inc=1, device_id={"space": lax.rem(my + r, sps)}, device_id_type=MESH)

    wide = jnp.concatenate([tab_ref[...], jnp.zeros((ROWS, samples - NFFT), F32)], axis=1)
    for k in range(blocks):
        tallf[:, k, :] = pltpu.roll(wide, starts_ref[k] - me * samples, 1)
    tall[...] = jnp.concatenate(split3(tallf[...].reshape(ROWS * blocks, samples)), axis=0)

    owners = [owner_ref[f] for f in range(NF)]
    slot_of = []
    for f in range(NF):
        rank = jnp.int32(0)
        for g in range(f):
            rank = rank + jnp.where(owners[g] == owners[f], 1, 0)
        slot_of.append(owners[f] * FCAP + rank)
    freq_in = []
    for slot in range(tms * FCAP):
        freq = jnp.int32(NF)
        for f in range(NF):
            freq = jnp.where(slot_of[f] == slot, f, freq)
        freq_in.append(freq)
    spec[NF] = jnp.zeros(spec.shape[1:], F32)
    gacc[...] = jnp.zeros(gacc.shape, F32)
    bd[...] = jnp.zeros(bd.shape, F32)

    order = [2, 1, 3] if tms == 4 else list(range(1, tms))
    m = ROWS * blocks
    sends = {}
    for q in range(quarters):
        loads[q].wait()
        s1, s2, s3 = split3(snap[q])
        p1 = mm(tall[...], s1)
        p2 = mm(tall[: 2 * m], s2)
        p3 = mm(tall[:m], s3)
        spectrum = p1[:m] + ((p1[m : 2 * m] + p2[:m]) + ((p1[2 * m :] + p2[m:]) + p3))
        for f in range(NF):
            for c in range(2):
                at = (2 * f + c) * blocks
                spec[f, :, c * QP : (c + 1) * QP] = spectrum[at : at + blocks]
        for peer in range(tms):
            for s in range(FCAP):
                send[q, peer, s] = spec[freq_in[peer * FCAP + s]]
        recv[q, me] = send[q, me]
        if q == 0:
            pl.semaphore_wait(barrier, tms + sps - 2)
        for r in order:
            peer = lax.rem(me + r, tms)
            sends[q, r] = pltpu.make_async_remote_copy(
                src_ref=send.at[q, peer], dst_ref=recv.at[q, me],
                send_sem=a2a_send.at[q, r], recv_sem=a2a_recv.at[q, r],
                device_id={"tm": peer}, device_id_type=MESH,
            )
            sends[q, r].start()

    def reduce_and_factor(turn):
        for s in range(FCAP):
            sl = pl.ds(s * nb, nb)
            packed[turn, s] = pack(gacc[sl, sl])
        for s in range(FCAP):
            worker = first_worker + s

            @pl.when(my != worker)
            def _():
                pltpu.make_async_remote_copy(
                    src_ref=packed.at[turn, s], dst_ref=gbuf.at[turn, my],
                    send_sem=g_send.at[turn, s], recv_sem=g_recv.at[turn, my],
                    device_id={"space": worker}, device_id_type=MESH,
                ).start()

        @pl.when((my >= first_worker) & (my < first_worker + FCAP))
        def _():
            mine = my - first_worker
            gbuf[turn, my] = packed[turn, mine]
            for r in range(1, sps):
                source = lax.rem(my + r, sps)
                pltpu.make_async_remote_copy(
                    src_ref=packed.at[turn, 0], dst_ref=gbuf.at[turn, source],
                    send_sem=g_send.at[turn, 0], recv_sem=g_recv.at[turn, source],
                    device_id={"space": source}, device_id_type=MESH,
                ).wait_recv()
            total = gbuf[turn, 0]
            for source in range(1, sps):
                total = total + gbuf[turn, source]
            inverse = pack(inverse_factor(unpack(total) / rows_total))
            pinv[turn] = inverse
            ibuf[turn, mine] = inverse
            copies = []
            for r in range(1, sps):
                peer = lax.rem(my + r, sps)
                copies.append(
                    pltpu.make_async_remote_copy(
                        src_ref=pinv.at[turn], dst_ref=ibuf.at[turn, mine],
                        send_sem=i_send.at[turn, r], recv_sem=i_recv.at[turn, mine],
                        device_id={"space": peer}, device_id_type=MESH,
                    )
                )
                copies[-1].start()
            for copy in copies:
                copy.wait_send()

        for s in range(FCAP):
            worker = first_worker + s

            @pl.when(my != worker)
            def _():
                pltpu.make_async_remote_copy(
                    src_ref=packed.at[turn, s], dst_ref=ibuf.at[turn, s],
                    send_sem=g_send.at[turn, s], recv_sem=i_recv.at[turn, s],
                    device_id={"space": worker}, device_id_type=MESH,
                ).wait()

            bd[s * nb : (s + 1) * nb, s * nb : (s + 1) * nb] = unpack(ibuf[turn, s])

    size = FCAP * nb
    for q in range(quarters):
        for r in order:
            sends[q, r].wait_recv()
        stacked = jnp.concatenate(
            [recv[q, :, s].reshape(nb, 2 * QP) for s in range(FCAP)], axis=0
        )
        x1, x2, x3 = split3(stacked)
        xs[q, 0], xs[q, 1], xs[q, 2] = x1, x2, x3
        p1 = mm_t(xs[q].reshape(3 * size, 2 * QP), x1)
        p2 = mm_t(xs[q, :2].reshape(2 * size, 2 * QP), x2)
        p3 = mm_t(x1, x3)
        gacc[...] += p1[:size] + (
            (p1[size : 2 * size] + p2[:size]) + ((p1[2 * size :] + p2[size:]) + p3)
        )
    reduce_and_factor(0)

    d1, d2, d3 = split3(bd[...])
    d321 = jnp.concatenate([d1, d2, d3], axis=0)
    gacc[...] = jnp.zeros(gacc.shape, F32)
    for q in range(quarters):
        p1 = mm(d321, xs[q, 0])
        p2 = mm(d321[: 2 * size], xs[q, 1])
        p3 = mm(d1, xs[q, 2])
        basis = p1[:size] + (
            (p1[size : 2 * size] + p2[:size]) + ((p1[2 * size :] + p2[size:]) + p3)
        )
        b1, b2 = split2(basis)
        bs[q, 0], bs[q, 1] = b1, b2
        p1 = mm_t(bs[q].reshape(2 * size, 2 * QP), b1)
        gacc[...] += p1[:size] + (p1[size:] + mm_t(b1, b2))
    reduce_and_factor(1)

    d1, d2 = split2(bd[...])
    d21 = jnp.concatenate([d1, d2], axis=0)
    for q in range(quarters):
        p1 = mm(d21, bs[q, 0])
        out_ref[q] = p1[:size] + (p1[size:] + mm(d1, bs[q, 1]))
    for q in range(quarters):
        for r in order:
            sends[q, r].wait_send()


def local(tms, sps, snapshots, block_starts, owner):
    samples, points = snapshots.shape
    blocks = block_starts.shape[0]
    nb = blocks * tms
    size = FCAP * nb
    quarters = points // QP
    table = jnp.asarray(dft_table())
    vm = pltpu.VMEM
    dma = pltpu.SemaphoreType.DMA
    out = pl.pallas_call(
        functools.partial(kernel, tms, sps),
        out_shape=jax.ShapeDtypeStruct((quarters, size, 2 * QP), F32),
        in_specs=[
            pl.BlockSpec(memory_space=pltpu.SMEM),
            pl.BlockSpec(memory_space=pltpu.SMEM),
            pl.BlockSpec(memory_space=pltpu.VMEM),
            pl.BlockSpec(memory_space=pl.ANY),
        ],
        out_specs=pl.BlockSpec(memory_space=pltpu.VMEM),
        scratch_shapes=[
            vm((quarters, samples, QP), F32),
            vm((ROWS, blocks, samples), F32),
            vm((3 * ROWS * blocks, samples), BF16),
            vm((NF + 1, blocks, 2 * QP), F32),
            vm((quarters, tms, FCAP, blocks, 2 * QP), F32),
            vm((quarters, tms, FCAP, blocks, 2 * QP), F32),
            vm((quarters, 3, size, 2 * QP), BF16),
            vm((quarters, 2, size, 2 * QP), BF16),
            vm((size, size), F32),
            vm((2, FCAP, nb // 4, nb * 4), F32),
            vm((2, sps, nb // 4, nb * 4), F32),
            vm((2, nb // 4, nb * 4), F32),
            vm((2, FCAP, nb // 4, nb * 4), F32),
            vm((size, size), F32),
            dma((quarters,)),
            dma((quarters, tms)),
            dma((quarters, tms)),
            dma((2, FCAP)),
            dma((2, sps)),
            dma((2, sps)),
            dma((2, FCAP)),
        ],
        compiler_params=pltpu.CompilerParams(
            collective_id=0, has_side_effects=True, vmem_limit_bytes=48 * 1024 * 1024
        ),
    )(block_starts, owner, table, snapshots)
    out = out.reshape(quarters, FCAP, nb, 2, QP).transpose(1, 2, 3, 0, 4)
    return out.reshape(FCAP, nb, 2, points)


def solution(mesh):
    placed = (P("tm", "space"), P("tm"), P())
    return jax.shard_map(
        functools.partial(local, mesh.shape["tm"], mesh.shape["space"]),
        mesh=mesh, in_specs=placed, out_specs=P("tm", None, None, "space"), check_vma=False,
    )
```

time: 196 us -> 51.6 us (0.26)
  blocking collectives: 73.2 us -> 0 us
  other arithmetic: 56.8 us -> 0 us
  Pallas kernels: 0 us -> 44.6 us
  local copies, waits for them, and re-layouts: 25.1 us -> 6.75 us
  waiting for transfers between devices: 17.2 us -> 0 us
  matrix products: 14 us -> 0 us
  between operations: 5.13 us -> 0.02 us
  starting transfers between devices: 4.24 us -> 0 us
    psum x2 -> x0, blocking collectives: 73.2 us -> none  [local(): totals = lax.psum(partial_sums, 'space')]
    another operation x12 -> x0, other arithmetic: 54.4 us -> none  [the longest x7 29.6 us: finish_pass(): factor = jnp.linalg.cholesky(gram)]
    pallas_call x0 -> x1, Pallas kernels: none -> 44.6 us  [local(): pl.pallas_call(functools.partial(kernel, tms, sps), out_shape=jax.ShapeDt...]
    all_to_all x1 -> x0, waiting for transfers between devices: 17.2 us -> none  [local(): lax.all_to_all(outgoing, 'tm', split_axis=0, concat_axis=2, tiled=True)]
    dot_general x6 -> x0, matrix products: 13.3 us -> none  [the longest x1 7.49 us: local(): jnp.einsum('fct,btp->fbcp', table, segments, precision=lax.Precision.HIGH...]
    unnamed x7 -> x8, local copies, waits for them, and re-layouts: 16.8 us -> 4.38 us
    all_to_all x1 -> x0, starting transfers between devices: 4.24 us -> none  [local(): lax.all_to_all(outgoing, 'tm', split_axis=0, concat_axis=2, tiled=True)]
    another operation x1 -> x0, local copies, waits for them, and re-layouts: 2.37 us -> none  [local(): jnp.stack([lax.dynamic_slice_in_dim(snapshots, block_starts[block] - offs...]
  transfers between devices with their start and end apart: 1 -> 0, of which waited for: 1 -> 0; matrix products, arithmetic and copies ran while one was open for 0% -> 0% of each run, Pallas kernels for 0% -> 0%
where the time goes in v1:
time: 51.6 us; the launch traced here: 51.3 us
  Pallas kernels  44.6 us (86%)
  local copies, waits for them, and re-layouts  6.75 us (13%)
    pallas_call x1, Pallas kernels, local(): pl.pallas_call(functools.partial(kernel, tms, sps), out_shape=jax.ShapeDt...  44.6 us
    unnamed x8, local copies, waits for them, and re-layouts  4.38 us
    reshape x1, local copies, waits for them, and re-layouts, local(): return out.reshape(FCAP, nb, 2, points)  1.53 us

profile of v1, /device:TPU:0, one launch (start us, length us, event | category | flops | bytes accessed | tf_op | source)
XLA Modules:
  0.0 51.3 jit_solution(6403106809033195623)
XLA Ops:
  0.0 0.0 copy-start
  0.0 2.3 %copy-done = f32[1152,1024]{1,0:T(8,128)S(1)} copy-done((f32[1152,1024]{1,0:T(8,128)S(1)}, f32[1152,1024]{1,0:T(8,128)}, u32[]{:S(2)}) %copy-start) | copy-done | bytes 4718616
  2.3 0.0 copy-start.1
  2.3 0.7 %copy-done.1 = f32[18,256]{1,0:T(8,128)S(1)} copy-done((f32[18,256]{1,0:T(8,128)S(1)}, f32[18,256]{1,0:T(8,128)}, u32[]{:S(2)}) %copy-start.1) | copy-done | bytes 18456
  3.1 0.0 copy-start.2
  3.1 0.7 %copy-done.2 = s32[8]{0:T(128)S(1)} copy-done((s32[8]{0:T(128)S(1)}, s32[8]{0:T(128)}, u32[]{:S(2)}) %copy-start.2) | copy-done | bytes 56
  3.7 0.0 copy-start.3
  3.7 0.7 %copy-done.3 = s32[9]{0:T(128)S(1)} copy-done((s32[9]{0:T(128)S(1)}, s32[9]{0:T(128)}, u32[]{:S(2)}) %copy-start.3) | copy-done | bytes 60
  4.4 44.6 %shard_map.46 = f32[4,160,512]{2,1,0:T(8,128)S(1)} custom-call(s32[8]{0:T(128)S(1)} %copy-done.2, s32[9]{0:T(128)S(1)} %copy-done.3, f32[18,256]{1,0:T(8,128)S(1)} %copy-done.1, f32[1152,1024]{1,0:T(8,128)S(1)} %copy-done), custom_call_target="tpu_custom_call" | custom-call | tf_op jit(solution)/shard_map/pallas_call | solution.py:274
  48.9 0.8 %reshape.6 = f32[4,5,32,2,256]{4,3,2,1,0:T(2,128)S(1)} reshape(f32[4,160,512]{2,1,0:T(8,128)S(1)} %shard_map.46) | data formatting | bytes 2621440 | tf_op jit(solution)/shard_map/reshape | solution.py:311
  49.8 1.5 %copy.6 = f32[4,5,32,1,2,256]{5,4,0,3,2,1:T(2,128)} copy(f32[4,5,32,1,2,256]{5,4,3,2,1,0:T(2,128)S(1)} %bitcast.3) | data formatting | bytes 2621440 | tf_op jit(solution)/shard_map/reshape | solution.py:312
Async XLA Ops:
  0.0 2.3 %copy-start = (f32[1152,1024]{1,0:T(8,128)S(1)}, f32[1152,1024]{1,0:T(8,128)}, u32[]{:S(2)}) copy-start(f32[1152,1024]{1,0:T(8,128)} %snap_hbm.1) | copy-start | bytes 14155780
  2.3 0.7 %copy-start.1 = (f32[18,256]{1,0:T(8,128)S(1)}, f32[18,256]{1,0:T(8,128)}, u32[]{:S(2)}) copy-start(f32[18,256]{1,0:T(8,128)} %constant.2.clone.tab_ref) | copy-start | bytes 55300
  3.1 0.7 %copy-start.2 = (s32[8]{0:T(128)S(1)}, s32[8]{0:T(128)}, u32[]{:S(2)}) copy-start(s32[8]{0:T(128)} %starts_ref.1) | copy-start | bytes 100
  3.7 0.7 %copy-start.3 = (s32[9]{0:T(128)S(1)}, s32[9]{0:T(128)}, u32[]{:S(2)}) copy-start(s32[9]{0:T(128)} %owner_ref.1) | copy-start | bytes 112

commit v2 on v1

--- a/solution.py
+++ b/solution.py
@@ -11,6 +11,7 @@
 NFFT = 256
 NF = 9
 FCAP = 5
+PAIR_CAP = 7
 ROWS = 2 * NF
 QP = 256
 F32 = jnp.float32
@@ -85,18 +86,31 @@
 
 
 def kernel(
-    tms, sps, starts_ref, owner_ref, tab_ref, snap_hbm, out_ref,
-    snap, tallf, tall, spec, send, recv, xs, bs, gacc, packed, gbuf, pinv, ibuf, bd,
-    snap_sem, a2a_send, a2a_recv, g_send, g_recv, i_send, i_recv,
+    tms, sps, starts_hbm, owner_hbm, tab_hbm, snap_hbm, out_ref,
+    starts_ref, owner_ref, tab_ref, snap, tallf, tall, spec, near, far, sib_in, xbuf,
+    xs, bs, gacc, packed, gbuf, pinv, ibuf, bd,
+    in_sem, snap_sem, a2a_send, a2a_recv, g_send, g_recv, i_send, i_recv, *far_in,
 ):
     quarters, samples = snap.shape[0], snap.shape[1]
-    blocks = starts_ref.shape[0]
+    blocks = starts_hbm.shape[0]
     nb = blocks * tms
     rows_total = 2.0 * quarters * QP * sps
     me = lax.axis_index("tm")
     my = lax.axis_index("space")
     first_worker = sps // 4
-
+    pair, half = me // 2, me % 2
+    sibling = 2 * pair + (1 - half)
+    across = 2 * (1 - pair) + half
+    across_sibling = 2 * (1 - pair) + (1 - half)
+
+    small = [
+        pltpu.make_async_copy(source, target, in_sem.at[i])
+        for i, (source, target) in enumerate(
+            [(starts_hbm, starts_ref), (owner_hbm, owner_ref), (tab_hbm, tab_ref)]
+        )
+    ]
+    for load in small:
+        load.start()
     loads = [
         pltpu.make_async_copy(snap_hbm.at[:, pl.ds(q * QP, QP)], snap.at[q], snap_sem.at[q])
         for q in range(quarters)
@@ -104,10 +118,12 @@
     for load in loads:
         load.start()
     barrier = pltpu.get_barrier_semaphore()
-    for r in range(1, tms):
-        pl.semaphore_signal(barrier, inc=1, device_id={"tm": lax.rem(me + r, tms)}, device_id_type=MESH)
+    for peer in (sibling, across):
+        pl.semaphore_signal(barrier, inc=1, device_id={"tm": peer}, device_id_type=MESH)
     for r in range(1, sps):
         pl.semaphore_signal(barrier, inc=1, device_id={"space": lax.rem(my + r, sps)}, device_id_type=MESH)
+    for load in small:
+        load.wait()
 
     wide = jnp.concatenate([tab_ref[...], jnp.zeros((ROWS, samples - NFFT), F32)], axis=1)
     for k in range(blocks):
@@ -115,25 +131,45 @@
     tall[...] = jnp.concatenate(split3(tallf[...].reshape(ROWS * blocks, samples)), axis=0)
 
     owners = [owner_ref[f] for f in range(NF)]
-    slot_of = []
+    owner_pair = [jnp.where(owners[f] >= 2, 1, 0) for f in range(NF)]
+    rank, pair_rank = [], []
     for f in range(NF):
-        rank = jnp.int32(0)
-        for g in range(f):
-            rank = rank + jnp.where(owners[g] == owners[f], 1, 0)
-        slot_of.append(owners[f] * FCAP + rank)
-    freq_in = []
-    for slot in range(tms * FCAP):
+        rank.append(sum([jnp.where(owners[g] == owners[f], 1, 0) for g in range(f)], jnp.int32(0)))
+        pair_rank.append(
+            sum([jnp.where(owner_pair[g] == owner_pair[f], 1, 0) for g in range(f)], jnp.int32(0))
+        )
+
+    def owned(holder, s):
+        freq, place = jnp.int32(NF), jnp.int32(0)
+        for f in range(NF):
+            hit = (owners[f] == holder) & (rank[f] == s)
+            freq = jnp.where(hit, f, freq)
+            place = jnp.where(hit, pair_rank[f], place)
+        return freq, place
+
+    mine = [owned(me, s) for s in range(FCAP)]
+    theirs = [owned(sibling, s)[0] for s in range(FCAP)]
+    distant = []
+    for place in range(PAIR_CAP):
         freq = jnp.int32(NF)
         for f in range(NF):
-            freq = jnp.where(slot_of[f] == slot, f, freq)
-        freq_in.append(freq)
+            freq = jnp.where((owner_pair[f] == 1 - pair) & (pair_rank[f] == place), f, freq)
+        distant.append(freq)
     spec[NF] = jnp.zeros(spec.shape[1:], F32)
     gacc[...] = jnp.zeros(gacc.shape, F32)
     bd[...] = jnp.zeros(bd.shape, F32)
 
-    order = [2, 1, 3] if tms == 4 else list(range(1, tms))
+    def hop(source, target, kind, q, peer):
+        return pltpu.make_async_remote_copy(
+            src_ref=source, dst_ref=target,
+            send_sem=a2a_send.at[q, kind], recv_sem=a2a_recv.at[q, kind],
+            device_id={"tm": peer}, device_id_type=MESH,
+        )
+
+    across_hops = [hop(far.at[q], far_in[q].at[0], 0, q, across) for q in range(quarters)]
+    sibling_hops = [hop(near.at[q, 1], sib_in.at[q], 1, q, sibling) for q in range(quarters)]
+    relays = [hop(far_in[q].at[0], far_in[q].at[1], 2, q, sibling) for q in range(quarters)]
     m = ROWS * blocks
-    sends = {}
     for q in range(quarters):
         loads[q].wait()
         s1, s2, s3 = split3(snap[q])
@@ -145,20 +181,15 @@
             for c in range(2):
                 at = (2 * f + c) * blocks
                 spec[f, :, c * QP : (c + 1) * QP] = spectrum[at : at + blocks]
-        for peer in range(tms):
-            for s in range(FCAP):
-                send[q, peer, s] = spec[freq_in[peer * FCAP + s]]
-        recv[q, me] = send[q, me]
+        for place in range(PAIR_CAP):
+            far[q, place] = spec[distant[place]]
         if q == 0:
-            pl.semaphore_wait(barrier, tms + sps - 2)
-        for r in order:
-            peer = lax.rem(me + r, tms)
-            sends[q, r] = pltpu.make_async_remote_copy(
-                src_ref=send.at[q, peer], dst_ref=recv.at[q, me],
-                send_sem=a2a_send.at[q, r], recv_sem=a2a_recv.at[q, r],
-                device_id={"tm": peer}, device_id_type=MESH,
-            )
-            sends[q, r].start()
+            pl.semaphore_wait(barrier, sps + 1)
+        across_hops[q].start()
+        for s in range(FCAP):
+            near[q, 0, s] = spec[mine[s][0]]
+            near[q, 1, s] = spec[theirs[s]]
+        sibling_hops[q].start()
 
     def reduce_and_factor(turn):
         for s in range(FCAP):
@@ -220,11 +251,22 @@
             bd[s * nb : (s + 1) * nb, s * nb : (s + 1) * nb] = unpack(ibuf[turn, s])
 
     size = FCAP * nb
-    for q in range(quarters):
-        for r in order:
-            sends[q, r].wait_recv()
+    across_hops[0].wait_recv()
+    relays[0].start()
+    for q in range(quarters):
+        if q + 1 < quarters:
+            across_hops[q + 1].wait_recv()
+            relays[q + 1].start()
+        sibling_hops[q].wait_recv()
+        relays[q].wait_recv()
+        xbuf[me] = near[q, 0]
+        xbuf[sibling] = sib_in[q]
+        for s in range(FCAP):
+            freq, place = mine[s]
+            xbuf[across, s] = jnp.where(freq < NF, far_in[q][0, place], 0.0)
+            xbuf[across_sibling, s] = jnp.where(freq < NF, far_in[q][1, place], 0.0)
         stacked = jnp.concatenate(
-            [recv[q, :, s].reshape(nb, 2 * QP) for s in range(FCAP)], axis=0
+            [xbuf[:, s].reshape(nb, 2 * QP) for s in range(FCAP)], axis=0
         )
         x1, x2, x3 = split3(stacked)
         xs[q, 0], xs[q, 1], xs[q, 2] = x1, x2, x3
@@ -256,10 +298,14 @@
     d21 = jnp.concatenate([d1, d2], axis=0)
     for q in range(quarters):
         p1 = mm(d21, bs[q, 0])
-        out_ref[q] = p1[:size] + (p1[size:] + mm(d1, bs[q, 1]))
-    for q in range(quarters):
-        for r in order:
-            sends[q, r].wait_send()
+        modes = p1[:size] + (p1[size:] + mm(d1, bs[q, 1]))
+        for s in range(FCAP):
+            for c in range(2):
+                part = modes[s * nb : (s + 1) * nb, c * QP : (c + 1) * QP]
+                out_ref[s, :, c, q * QP : (q + 1) * QP] = part
+    for q in range(quarters):
+        for copy in (across_hops[q], sibling_hops[q], relays[q]):
+            copy.wait_send()
 
 
 def local(tms, sps, snapshots, block_starts, owner):
@@ -271,23 +317,23 @@
     table = jnp.asarray(dft_table())
     vm = pltpu.VMEM
     dma = pltpu.SemaphoreType.DMA
-    out = pl.pallas_call(
+    return pl.pallas_call(
         functools.partial(kernel, tms, sps),
-        out_shape=jax.ShapeDtypeStruct((quarters, size, 2 * QP), F32),
-        in_specs=[
-            pl.BlockSpec(memory_space=pltpu.SMEM),
-            pl.BlockSpec(memory_space=pltpu.SMEM),
-            pl.BlockSpec(memory_space=pltpu.VMEM),
-            pl.BlockSpec(memory_space=pl.ANY),
-        ],
+        out_shape=jax.ShapeDtypeStruct((FCAP, nb, 2, points), F32),
+        in_specs=[pl.BlockSpec(memory_space=pltpu.HBM)] * 4,
         out_specs=pl.BlockSpec(memory_space=pltpu.VMEM),
         scratch_shapes=[
+            pltpu.SMEM((blocks,), jnp.int32),
+            pltpu.SMEM((NF,), jnp.int32),
+            vm((ROWS, NFFT), F32),
             vm((quarters, samples, QP), F32),
             vm((ROWS, blocks, samples), F32),
             vm((3 * ROWS * blocks, samples), BF16),
             vm((NF + 1, blocks, 2 * QP), F32),
-            vm((quarters, tms, FCAP, blocks, 2 * QP), F32),
-            vm((quarters, tms, FCAP, blocks, 2 * QP), F32),
+            vm((quarters, 2, FCAP, blocks, 2 * QP), F32),
+            vm((quarters, PAIR_CAP, blocks, 2 * QP), F32),
+            vm((quarters, FCAP, blocks, 2 * QP), F32),
+            vm((tms, FCAP, blocks, 2 * QP), F32),
             vm((quarters, 3, size, 2 * QP), BF16),
             vm((quarters, 2, size, 2 * QP), BF16),
             vm((size, size), F32),
@@ -296,20 +342,20 @@
             vm((2, nb // 4, nb * 4), F32),
             vm((2, FCAP, nb // 4, nb * 4), F32),
             vm((size, size), F32),
+            dma((3,)),
             dma((quarters,)),
-            dma((quarters, tms)),
-            dma((quarters, tms)),
+            dma((quarters, 3)),
+            dma((quarters, 3)),
             dma((2, FCAP)),
             dma((2, sps)),
             dma((2, sps)),
             dma((2, FCAP)),
+            *[vm((2, PAIR_CAP, blocks, 2 * QP), F32) for _ in range(quarters)],
         ],
         compiler_params=pltpu.CompilerParams(
-            collective_id=0, has_side_effects=True, vmem_limit_bytes=48 * 1024 * 1024
+            collective_id=0, has_side_effects=True, vmem_limit_bytes=64 * 1024 * 1024 - 65536
         ),
     )(block_starts, owner, table, snapshots)
-    out = out.reshape(quarters, FCAP, nb, 2, QP).transpose(1, 2, 3, 0, 4)
-    return out.reshape(FCAP, nb, 2, points)
 
 
 def solution(mesh):

time: 51.6 us -> 46.1 us (0.89)
  local copies, waits for them, and re-layouts: 6.75 us -> 2.86 us
  Pallas kernels: 44.6 us -> 43.1 us
    reshape x2 -> x0, local copies, waits for them, and re-layouts: 2.37 us -> none  [the longest x1 1.53 us: local(): return out.reshape(FCAP, nb, 2, points)]
    unnamed x8 -> x1, local copies, waits for them, and re-layouts: 4.38 us -> 2.86 us
    pallas_call x1, Pallas kernels: 44.6 us -> 43.1 us  [local(): pl.pallas_call(functools.partial(kernel, tms, sps), out_shape=jax.ShapeDt...]
where the time goes in v2:
time: 46.1 us; the launch traced here: 46 us
  Pallas kernels  43.1 us (93%)
  local copies, waits for them, and re-layouts  2.86 us (6%)
    pallas_call x1, Pallas kernels, local(): pl.pallas_call(functools.partial(kernel, tms, sps), out_shape=jax.ShapeDt...  43.1 us
    unnamed x1, local copies, waits for them, and re-layouts  2.86 us

profile of v2, /device:TPU:0, one launch (start us, length us, event | category | flops | bytes accessed | tf_op | source)
XLA Modules:
  0.0 46.0 jit_solution(1482013254303906552)
XLA Ops:
  0.0 43.1 %shard_map.46 = f32[5,32,2,1024]{3,2,1,0:T(2,128)} custom-call(s32[8]{0:T(128)} %starts_hbm.1, s32[9]{0:T(128)} %owner_hbm.1, f32[18,256]{1,0:T(8,128)} %constant.2.clone.tab_hbm, f32[1152,1024]{1,0:T(8,128)} %snap_hbm.1), custom_call_target="tpu_custom_call" | custom-call | tf_op jit(solution)/shard_map/pallas_call | solution.py:320
  43.1 2.9 %copy.6 = f32[5,32,2,1024]{3,2,1,0:T(2,128)} copy(f32[5,32,2,1024]{3,2,1,0:T(2,128)} %shard_map.46) | data formatting | bytes 2621440

commit v3 on v2

--- a/solution.py
+++ b/solution.py
@@ -12,6 +12,8 @@
 NF = 9
 FCAP = 5
 PAIR_CAP = 7
+GAP = 112
+VMEM_BYTES = 64 * 1024 * 1024 - 65536
 ROWS = 2 * NF
 QP = 256
 F32 = jnp.float32
@@ -78,7 +80,7 @@
             k = first + j
             pivot = jnp.broadcast_to(cols[j][k : k + 1], (n, 128))
             diag = jnp.where(rows == k, pivot, diag)
-            factor = jnp.where(rows > k, cols[j] / pivot, 0.0)
+            factor = jnp.where(rows > k, cols[j] * (1.0 / cols[j][k : k + 1]), 0.0)
             work = work - factor * work[k : k + 1]
             for i in range(j + 1, panel):
                 cols[i] = cols[i] - factor * cols[i][k : k + 1]
@@ -86,7 +88,7 @@
 
 
 def kernel(
-    tms, sps, starts_hbm, owner_hbm, tab_hbm, snap_hbm, out_ref,
+    tms, sps, starts_hbm, owner_hbm, tab_hbm, snap_hbm, basis_out, factor_out,
     starts_ref, owner_ref, tab_ref, snap, tallf, tall, spec, near, far, sib_in, xbuf,
     xs, bs, gacc, packed, gbuf, pinv, ibuf, bd,
     in_sem, snap_sem, a2a_send, a2a_recv, g_send, g_recv, i_send, i_recv, *far_in,
@@ -122,12 +124,17 @@
         pl.semaphore_signal(barrier, inc=1, device_id={"tm": peer}, device_id_type=MESH)
     for r in range(1, sps):
         pl.semaphore_signal(barrier, inc=1, device_id={"space": lax.rem(my + r, sps)}, device_id_type=MESH)
+    tallf[...] = jnp.zeros(tallf.shape, F32)
     for load in small:
         load.wait()
 
-    wide = jnp.concatenate([tab_ref[...], jnp.zeros((ROWS, samples - NFFT), F32)], axis=1)
+    span = 2 * NFFT
+    wide = jnp.concatenate([tab_ref[...], jnp.zeros((ROWS, span - NFFT), F32)], axis=1)
     for k in range(blocks):
-        tallf[:, k, :] = pltpu.roll(wide, starts_ref[k] - me * samples, 1)
+        base = k * GAP // 128 * 128
+        keep = min(span, samples - base)
+        moved = pltpu.roll(wide, starts_ref[k] - me * samples - base, 1)
+        tallf[:, k, base : base + keep] = moved[:, :keep]
     tall[...] = jnp.concatenate(split3(tallf[...].reshape(ROWS * blocks, samples)), axis=0)
 
     owners = [owner_ref[f] for f in range(NF)]
@@ -248,7 +255,10 @@
                     device_id={"space": worker}, device_id_type=MESH,
                 ).wait()
 
-            bd[s * nb : (s + 1) * nb, s * nb : (s + 1) * nb] = unpack(ibuf[turn, s])
+            if turn == 0:
+                bd[s * nb : (s + 1) * nb, s * nb : (s + 1) * nb] = unpack(ibuf[turn, s])
+            else:
+                factor_out[s] = ibuf[turn, s]
 
     size = FCAP * nb
     across_hops[0].wait_recv()
@@ -281,6 +291,9 @@
     d1, d2, d3 = split3(bd[...])
     d321 = jnp.concatenate([d1, d2, d3], axis=0)
     gacc[...] = jnp.zeros(gacc.shape, F32)
+    stores = [
+        pltpu.make_async_copy(bs.at[q], basis_out.at[q], snap_sem.at[q]) for q in range(quarters)
+    ]
     for q in range(quarters):
         p1 = mm(d321, xs[q, 0])
         p2 = mm(d321[: 2 * size], xs[q, 1])
@@ -290,22 +303,34 @@
         )
         b1, b2 = split2(basis)
         bs[q, 0], bs[q, 1] = b1, b2
+        stores[q].start()
         p1 = mm_t(bs[q].reshape(2 * size, 2 * QP), b1)
         gacc[...] += p1[:size] + (p1[size:] + mm_t(b1, b2))
     reduce_and_factor(1)
 
-    d1, d2 = split2(bd[...])
-    d21 = jnp.concatenate([d1, d2], axis=0)
-    for q in range(quarters):
-        p1 = mm(d21, bs[q, 0])
-        modes = p1[:size] + (p1[size:] + mm(d1, bs[q, 1]))
-        for s in range(FCAP):
-            for c in range(2):
-                part = modes[s * nb : (s + 1) * nb, c * QP : (c + 1) * QP]
-                out_ref[s, :, c, q * QP : (q + 1) * QP] = part
+    for store in stores:
+        store.wait()
     for q in range(quarters):
         for copy in (across_hops[q], sibling_hops[q], relays[q]):
             copy.wait_send()
+
+
+def finish_kernel(factor_ref, basis_ref, out_ref, bd):
+    nb = out_ref.shape[1]
+    size = FCAP * nb
+
+    @pl.when(pl.program_id(0) == 0)
+    def _():
+        bd[...] = jnp.zeros(bd.shape, F32)
+        for s in range(FCAP):
+            bd[s * nb : (s + 1) * nb, s * nb : (s + 1) * nb] = unpack(factor_ref[s])
+
+    d1, d2 = split2(bd[...])
+    p1 = mm(jnp.concatenate([d1, d2], axis=0), basis_ref[0, 0])
+    modes = p1[:size] + (p1[size:] + mm(d1, basis_ref[0, 1]))
+    for s in range(FCAP):
+        for c in range(2):
+            out_ref[s, :, c, :] = modes[s * nb : (s + 1) * nb, c * QP : (c + 1) * QP]
 
 
 def local(tms, sps, snapshots, block_starts, owner):
@@ -317,11 +342,17 @@
     table = jnp.asarray(dft_table())
     vm = pltpu.VMEM
     dma = pltpu.SemaphoreType.DMA
-    return pl.pallas_call(
+    basis, factors = pl.pallas_call(
         functools.partial(kernel, tms, sps),
-        out_shape=jax.ShapeDtypeStruct((FCAP, nb, 2, points), F32),
+        out_shape=[
+            jax.ShapeDtypeStruct((quarters, 2, size, 2 * QP), BF16),
+            jax.ShapeDtypeStruct((FCAP, nb // 4, nb * 4), F32),
+        ],
         in_specs=[pl.BlockSpec(memory_space=pltpu.HBM)] * 4,
-        out_specs=pl.BlockSpec(memory_space=pltpu.VMEM),
+        out_specs=[
+            pl.BlockSpec(memory_space=pltpu.HBM),
+            pl.BlockSpec(memory_space=pltpu.VMEM),
+        ],
         scratch_shapes=[
             pltpu.SMEM((blocks,), jnp.int32),
             pltpu.SMEM((NF,), jnp.int32),
@@ -353,9 +384,21 @@
             *[vm((2, PAIR_CAP, blocks, 2 * QP), F32) for _ in range(quarters)],
         ],
         compiler_params=pltpu.CompilerParams(
-            collective_id=0, has_side_effects=True, vmem_limit_bytes=64 * 1024 * 1024 - 65536
+            collective_id=0, has_side_effects=True, vmem_limit_bytes=VMEM_BYTES
         ),
     )(block_starts, owner, table, snapshots)
+    return pl.pallas_call(
+        finish_kernel,
+        grid=(quarters,),
+        out_shape=jax.ShapeDtypeStruct((FCAP, nb, 2, points), F32),
+        in_specs=[
+            pl.BlockSpec((FCAP, nb // 4, nb * 4), lambda q: (0, 0, 0)),
+            pl.BlockSpec((1, 2, size, 2 * QP), lambda q: (q, 0, 0, 0)),
+        ],
+        out_specs=pl.BlockSpec((FCAP, nb, 2, QP), lambda q: (0, 0, 0, q)),
+        scratch_shapes=[vm((size, size), F32)],
+        compiler_params=pltpu.CompilerParams(vmem_limit_bytes=VMEM_BYTES),
+    )(factors, basis)
 
 
 def solution(mesh):

time: 46.1 us -> 46 us (level)
  local copies, waits for them, and re-layouts: 2.86 us -> 0 us
  Pallas kernels: 43.1 us -> 45.8 us
    unnamed x1 -> x0, local copies, waits for them, and re-layouts: 2.86 us -> none
    pallas_call x1 -> x2, Pallas kernels: 43.1 us -> 45.8 us  [the longest x1 41.6 us: local(): pl.pallas_call(functools.partial(kernel, tms, sps), out_shape=[jax.ShapeD...]
where the time goes in v3:
time: 46 us; the launch traced here: 45.8 us
  Pallas kernels  45.8 us (100%)
    pallas_call x1, Pallas kernels, local(): pl.pallas_call(functools.partial(kernel, tms, sps), out_shape=[jax.ShapeD...  41.6 us
    pallas_call x1, Pallas kernels, local(): pl.pallas_call(finish_kernel, grid=(quarters,), out_shape=jax.ShapeDtypeS...  4.24 us

profile of v3, /device:TPU:0, one launch (start us, length us, event | category | flops | bytes accessed | tf_op | source)
XLA Modules:
  0.0 45.8 jit_solution(3890928456560540987)
XLA Ops:
  0.0 41.6 %shard_map.46 = (bf16[4,2,160,512]{3,2,1,0:T(8,128)(2,1)}, f32[5,8,128]{2,1,0:T(8,128)}) custom-call(s32[8]{0:T(128)} %starts_hbm.1, s32[9]{0:T(128)} %owner_hbm.1, f32[18,256]{1,0:T(8,128)} %constant.2.clone.tab_hbm, f32[1152,1024]{1,0:T(8,128)} %snap_hbm.1), custom_call_target="tpu_custom_call" | custom-call | tf_op jit(solution)/shard_map/pallas_call | solution.py:345
  41.6 4.2 %shard_map.47 = f32[5,32,2,1024]{3,2,1,0:T(2,128)} custom-call(f32[5,8,128]{2,1,0:T(8,128)} %get-tuple-element.7.factor_ref, bf16[4,2,160,512]{3,2,1,0:T(8,128)(2,1)} %get-tuple-element.8.basis_ref), custom_call_target="tpu_custom_call" | custom-call | tf_op jit(solution)/shard_map/pallas_call | solution.py:390

commit v4 on v3

--- a/solution.py
+++ b/solution.py
@@ -61,13 +61,12 @@
     return jnp.concatenate([packed[:, n * i : n * i + n] for i in range(4)], axis=0)
 
 
-def inverse_factor(gram, panel=8):
+def inverse_factor(gram, empty, panel=8):
     n = gram.shape[0]
     row = lax.broadcasted_iota(jnp.int32, (n, n), 0)
     col = lax.broadcasted_iota(jnp.int32, (n, n), 1)
     eye = jnp.where(row == col, 1.0, 0.0).astype(F32)
-    trace = jnp.sum(jnp.sum(gram * eye, axis=1, keepdims=True), axis=0, keepdims=True)
-    gram = gram + jnp.where(trace == 0.0, 1.0, 0.0) * eye
+    gram = gram + jnp.where(empty, 1.0, 0.0) * eye
     work = jnp.concatenate([eye, gram, jnp.zeros((n, 128 - 2 * n), F32)], axis=1)
     rows = lax.broadcasted_iota(jnp.int32, (n, 128), 0)
     diag = jnp.ones((n, 128), F32)
@@ -154,7 +153,7 @@
             place = jnp.where(hit, pair_rank[f], place)
         return freq, place
 
-    mine = [owned(me, s) for s in range(FCAP)]
+    held = [owned(me, s) for s in range(FCAP)]
     theirs = [owned(sibling, s)[0] for s in range(FCAP)]
     distant = []
     for place in range(PAIR_CAP):
@@ -194,7 +193,7 @@
             pl.semaphore_wait(barrier, sps + 1)
         across_hops[q].start()
         for s in range(FCAP):
-            near[q, 0, s] = spec[mine[s][0]]
+            near[q, 0, s] = spec[held[s][0]]
             near[q, 1, s] = spec[theirs[s]]
         sibling_hops[q].start()
 
@@ -227,7 +226,11 @@
             total = gbuf[turn, 0]
             for source in range(1, sps):
                 total = total + gbuf[turn, source]
-            inverse = pack(inverse_factor(unpack(total) / rows_total))
+            freq = held[0][0]
+            for s in range(1, FCAP):
+                freq = jnp.where(mine == s, held[s][0], freq)
+            empty = freq == NF
+            inverse = pack(inverse_factor(unpack(total * (1.0 / rows_total)), empty))
             pinv[turn] = inverse
             ibuf[turn, mine] = inverse
             copies = []
@@ -272,7 +275,7 @@
         xbuf[me] = near[q, 0]
         xbuf[sibling] = sib_in[q]
         for s in range(FCAP):
-            freq, place = mine[s]
+            freq, place = held[s]
             xbuf[across, s] = jnp.where(freq < NF, far_in[q][0, place], 0.0)
             xbuf[across_sibling, s] = jnp.where(freq < NF, far_in[q][1, place], 0.0)
         stacked = jnp.concatenate(
@@ -315,22 +318,20 @@
             copy.wait_send()
 
 
-def finish_kernel(factor_ref, basis_ref, out_ref, bd):
-    nb = out_ref.shape[1]
-    size = FCAP * nb
-
-    @pl.when(pl.program_id(0) == 0)
-    def _():
-        bd[...] = jnp.zeros(bd.shape, F32)
-        for s in range(FCAP):
-            bd[s * nb : (s + 1) * nb, s * nb : (s + 1) * nb] = unpack(factor_ref[s])
-
-    d1, d2 = split2(bd[...])
-    p1 = mm(jnp.concatenate([d1, d2], axis=0), basis_ref[0, 0])
-    modes = p1[:size] + (p1[size:] + mm(d1, basis_ref[0, 1]))
-    for s in range(FCAP):
+def finish_kernel(factor_ref, basis_ref, out_ref):
+    quarters = basis_ref.shape[0]
+    nb = basis_ref.shape[2]
+    tiles = quarters * QP // 128
+    d1, d2 = split2(unpack(factor_ref[0]))
+    d21 = jnp.concatenate([d1, d2], axis=0)
+    for q in range(quarters):
+        p1 = mm(d21, basis_ref[q, 0])
+        modes = p1[:nb] + (p1[nb:] + mm(d1, basis_ref[q, 1]))
         for c in range(2):
-            out_ref[s, :, c, :] = modes[s * nb : (s + 1) * nb, c * QP : (c + 1) * QP]
+            for t in range(QP // 128):
+                at = 2 * (q * (QP // 128) + t) + c
+                lane = c * QP + t * 128
+                out_ref[pl.ds(at, nb, stride=2 * tiles), :] = modes[:, lane : lane + 128]
 
 
 def local(tms, sps, snapshots, block_starts, owner):
@@ -387,18 +388,20 @@
             collective_id=0, has_side_effects=True, vmem_limit_bytes=VMEM_BYTES
         ),
     )(block_starts, owner, table, snapshots)
-    return pl.pallas_call(
+    tiles = points // 128
+    modes = pl.pallas_call(
         finish_kernel,
-        grid=(quarters,),
-        out_shape=jax.ShapeDtypeStruct((FCAP, nb, 2, points), F32),
+        grid=(FCAP,),
+        out_shape=jax.ShapeDtypeStruct((size * tiles * 2, 128), F32),
         in_specs=[
-            pl.BlockSpec((FCAP, nb // 4, nb * 4), lambda q: (0, 0, 0)),
-            pl.BlockSpec((1, 2, size, 2 * QP), lambda q: (q, 0, 0, 0)),
+            pl.BlockSpec((1, nb // 4, nb * 4), lambda s: (s, 0, 0)),
+            pl.BlockSpec((quarters, 2, nb, 2 * QP), lambda s: (0, 0, s, 0)),
         ],
-        out_specs=pl.BlockSpec((FCAP, nb, 2, QP), lambda q: (0, 0, 0, q)),
-        scratch_shapes=[vm((size, size), F32)],
+        out_specs=pl.BlockSpec((nb * tiles * 2, 128), lambda s: (s, 0)),
         compiler_params=pltpu.CompilerParams(vmem_limit_bytes=VMEM_BYTES),
     )(factors, basis)
+    modes = modes.reshape(FCAP, nb, tiles, 2, 128).transpose(0, 1, 3, 2, 4)
+    return modes.reshape(FCAP, nb, 2, points)
 
 
 def solution(mesh):

time: 46 us -> 46.5 us (1.011)
  Pallas kernels: 45.8 us -> 46.3 us
    pallas_call x1, Pallas kernels: 4.24 us -> 4.77 us  [local(): pl.pallas_call(finish_kernel, grid=(FCAP,), out_shape=jax.ShapeDtypeStruc...]
where the time goes in v4:
time: 46.5 us; the launch traced here: 46.3 us
  Pallas kernels  46.3 us (100%)
    pallas_call x1, Pallas kernels, local(): pl.pallas_call(functools.partial(kernel, tms, sps), out_shape=[jax.ShapeD...  41.5 us
    pallas_call x1, Pallas kernels, local(): pl.pallas_call(finish_kernel, grid=(FCAP,), out_shape=jax.ShapeDtypeStruc...  4.77 us

profile of v4, /device:TPU:0, one launch (start us, length us, event | category | flops | bytes accessed | tf_op | source)
XLA Modules:
  0.0 46.3 jit_solution(11846108396644665875)
XLA Ops:
  0.0 41.5 %shard_map.46 = (bf16[4,2,160,512]{3,2,1,0:T(8,128)(2,1)}, f32[5,8,128]{2,1,0:T(8,128)}) custom-call(s32[8]{0:T(128)} %starts_hbm.1, s32[9]{0:T(128)} %owner_hbm.1, f32[18,256]{1,0:T(8,128)} %constant.2.clone.tab_hbm, f32[1152,1024]{1,0:T(8,128)} %snap_hbm.1), custom_call_target="tpu_custom_call" | custom-call | tf_op jit(solution)/shard_map/pallas_call | solution.py:346
  41.5 4.8 %shard_map.47 = f32[2560,128]{1,0:T(8,128)} custom-call(f32[5,8,128]{2,1,0:T(8,128)} %get-tuple-element.7.factor_ref, bf16[4,2,160,512]{3,2,1,0:T(8,128)(2,1)} %get-tuple-element.8.basis_ref), custom_call_target="tpu_custom_call" | custom-call | tf_op jit(solution)/shard_map/pallas_call | solution.py:392

commit v5 on v4

--- a/solution.py
+++ b/solution.py
@@ -87,10 +87,10 @@
 
 
 def kernel(
-    tms, sps, starts_hbm, owner_hbm, tab_hbm, snap_hbm, basis_out, factor_out,
+    tms, sps, starts_hbm, owner_hbm, tab_hbm, snap_hbm, out_ref,
     starts_ref, owner_ref, tab_ref, snap, tallf, tall, spec, near, far, sib_in, xbuf,
-    xs, bs, gacc, packed, gbuf, pinv, ibuf, bd,
-    in_sem, snap_sem, a2a_send, a2a_recv, g_send, g_recv, i_send, i_recv, *far_in,
+    xs, bs, gacc, packed, gbuf, pinv, ibuf, bd, parts,
+    in_sem, snap_sem, a2a_send, a2a_recv, g_send, g_recv, i_send, i_recv, far_in, stage,
 ):
     quarters, samples = snap.shape[0], snap.shape[1]
     blocks = starts_hbm.shape[0]
@@ -112,12 +112,12 @@
     ]
     for load in small:
         load.start()
-    loads = [
-        pltpu.make_async_copy(snap_hbm.at[:, pl.ds(q * QP, QP)], snap.at[q], snap_sem.at[q])
-        for q in range(quarters)
-    ]
-    for load in loads:
-        load.start()
+    def snap_load(q):
+        lanes = pl.ds(pl.multiple_of(q * QP, QP), QP)
+        return pltpu.make_async_copy(snap_hbm.at[:, lanes], snap.at[q], snap_sem.at[q])
+
+    for q in range(quarters):
+        snap_load(q).start()
     barrier = pltpu.get_barrier_semaphore()
     for peer in (sibling, across):
         pl.semaphore_signal(barrier, inc=1, device_id={"tm": peer}, device_id_type=MESH)
@@ -172,12 +172,21 @@
             device_id={"tm": peer}, device_id_type=MESH,
         )
 
-    across_hops = [hop(far.at[q], far_in[q].at[0], 0, q, across) for q in range(quarters)]
-    sibling_hops = [hop(near.at[q, 1], sib_in.at[q], 1, q, sibling) for q in range(quarters)]
-    relays = [hop(far_in[q].at[0], far_in[q].at[1], 2, q, sibling) for q in range(quarters)]
+    def across_hop(q):
+        return hop(far.at[q], far_in.at[q, 0], 0, q, across)
+
+    def sibling_hop(q):
+        return hop(near.at[q, 1], sib_in.at[q], 1, q, sibling)
+
+    def relay(q):
+        return hop(far_in.at[q, 0], far_in.at[q, 1], 2, q, sibling)
+
     m = ROWS * blocks
-    for q in range(quarters):
-        loads[q].wait()
+    pl.semaphore_wait(barrier, sps + 1)
+
+    @pl.loop(0, quarters)
+    def _(q):
+        snap_load(q).wait()
         s1, s2, s3 = split3(snap[q])
         p1 = mm(tall[...], s1)
         p2 = mm(tall[: 2 * m], s2)
@@ -189,13 +198,11 @@
                 spec[f, :, c * QP : (c + 1) * QP] = spectrum[at : at + blocks]
         for place in range(PAIR_CAP):
             far[q, place] = spec[distant[place]]
-        if q == 0:
-            pl.semaphore_wait(barrier, sps + 1)
-        across_hops[q].start()
+        across_hop(q).start()
         for s in range(FCAP):
             near[q, 0, s] = spec[held[s][0]]
             near[q, 1, s] = spec[theirs[s]]
-        sibling_hops[q].start()
+        sibling_hop(q).start()
 
     def reduce_and_factor(turn):
         for s in range(FCAP):
@@ -258,26 +265,28 @@
                     device_id={"space": worker}, device_id_type=MESH,
                 ).wait()
 
-            if turn == 0:
-                bd[s * nb : (s + 1) * nb, s * nb : (s + 1) * nb] = unpack(ibuf[turn, s])
-            else:
-                factor_out[s] = ibuf[turn, s]
+            bd[s * nb : (s + 1) * nb, s * nb : (s + 1) * nb] = unpack(ibuf[turn, s])
 
     size = FCAP * nb
-    across_hops[0].wait_recv()
-    relays[0].start()
-    for q in range(quarters):
-        if q + 1 < quarters:
-            across_hops[q + 1].wait_recv()
-            relays[q + 1].start()
-        sibling_hops[q].wait_recv()
-        relays[q].wait_recv()
+    across_hop(0).wait_recv()
+    relay(0).start()
+
+    @pl.loop(0, quarters)
+    def _(q):
+        @pl.when(q + 1 < quarters)
+        def _():
+            across_hop(q + 1).wait_recv()
+            relay(q + 1).start()
+
+        sibling_hop(q).wait_recv()
         xbuf[me] = near[q, 0]
         xbuf[sibling] = sib_in[q]
+        relay(q).wait_recv()
+        stage[...] = far_in[q]
         for s in range(FCAP):
             freq, place = held[s]
-            xbuf[across, s] = jnp.where(freq < NF, far_in[q][0, place], 0.0)
-            xbuf[across_sibling, s] = jnp.where(freq < NF, far_in[q][1, place], 0.0)
+            xbuf[across, s] = jnp.where(freq < NF, stage[0, place], 0.0)
+            xbuf[across_sibling, s] = jnp.where(freq < NF, stage[1, place], 0.0)
         stacked = jnp.concatenate(
             [xbuf[:, s].reshape(nb, 2 * QP) for s in range(FCAP)], axis=0
         )
@@ -289,49 +298,62 @@
         gacc[...] += p1[:size] + (
             (p1[size : 2 * size] + p2[:size]) + ((p1[2 * size :] + p2[size:]) + p3)
         )
+
     reduce_and_factor(0)
 
     d1, d2, d3 = split3(bd[...])
-    d321 = jnp.concatenate([d1, d2, d3], axis=0)
+    parts[...] = jnp.concatenate([d1, d2, d3], axis=0)
     gacc[...] = jnp.zeros(gacc.shape, F32)
-    stores = [
-        pltpu.make_async_copy(bs.at[q], basis_out.at[q], snap_sem.at[q]) for q in range(quarters)
-    ]
-    for q in range(quarters):
-        p1 = mm(d321, xs[q, 0])
-        p2 = mm(d321[: 2 * size], xs[q, 1])
-        p3 = mm(d1, xs[q, 2])
+
+    @pl.loop(0, quarters)
+    def _(q):
+        p1 = mm(parts[...], xs[q, 0])
+        p2 = mm(parts[: 2 * size], xs[q, 1])
+        p3 = mm(parts[:size], xs[q, 2])
         basis = p1[:size] + (
             (p1[size : 2 * size] + p2[:size]) + ((p1[2 * size :] + p2[size:]) + p3)
         )
         b1, b2 = split2(basis)
         bs[q, 0], bs[q, 1] = b1, b2
-        stores[q].start()
         p1 = mm_t(bs[q].reshape(2 * size, 2 * QP), b1)
         gacc[...] += p1[:size] + (p1[size:] + mm_t(b1, b2))
+
     reduce_and_factor(1)
 
-    for store in stores:
-        store.wait()
-    for q in range(quarters):
-        for copy in (across_hops[q], sibling_hops[q], relays[q]):
-            copy.wait_send()
-
-
-def finish_kernel(factor_ref, basis_ref, out_ref):
-    quarters = basis_ref.shape[0]
-    nb = basis_ref.shape[2]
+    d1, d2 = split2(bd[...])
+    parts[: 2 * size] = jnp.concatenate([d1, d2], axis=0)
     tiles = quarters * QP // 128
-    d1, d2 = split2(unpack(factor_ref[0]))
-    d21 = jnp.concatenate([d1, d2], axis=0)
-    for q in range(quarters):
-        p1 = mm(d21, basis_ref[q, 0])
-        modes = p1[:nb] + (p1[nb:] + mm(d1, basis_ref[q, 1]))
+
+    @pl.loop(0, quarters)
+    def _(q):
+        p1 = mm(parts[: 2 * size], bs[q, 0])
+        modes = p1[:size] + (p1[size:] + mm(parts[:size], bs[q, 1]))
         for c in range(2):
             for t in range(QP // 128):
                 at = 2 * (q * (QP // 128) + t) + c
                 lane = c * QP + t * 128
-                out_ref[pl.ds(at, nb, stride=2 * tiles), :] = modes[:, lane : lane + 128]
+                out_ref[pl.ds(at, size, stride=2 * tiles), :] = modes[:, lane : lane + 128]
+
+    @pl.loop(0, quarters)
+    def _(q):
+        across_hop(q).wait_send()
+        sibling_hop(q).wait_send()
+        relay(q).wait_send()
+
+
+def hand_over(source, target, sem):
+    chunks = sem.shape[0]
+    rows = source.shape[0] // chunks
+    copies = [
+        pltpu.make_async_copy(
+            source.at[pl.ds(i * rows, rows)], target.at[pl.ds(i * rows, rows)], sem.at[i]
+        )
+        for i in range(chunks)
+    ]
+    for copy in copies:
+        copy.start()
+    for copy in copies:
+        copy.wait()
 
 
 def local(tms, sps, snapshots, block_starts, owner):
@@ -340,20 +362,15 @@
     nb = blocks * tms
     size = FCAP * nb
     quarters = points // QP
+    tiles = points // 128
     table = jnp.asarray(dft_table())
     vm = pltpu.VMEM
     dma = pltpu.SemaphoreType.DMA
-    basis, factors = pl.pallas_call(
+    modes = pl.pallas_call(
         functools.partial(kernel, tms, sps),
-        out_shape=[
-            jax.ShapeDtypeStruct((quarters, 2, size, 2 * QP), BF16),
-            jax.ShapeDtypeStruct((FCAP, nb // 4, nb * 4), F32),
-        ],
+        out_shape=jax.ShapeDtypeStruct((size * tiles * 2, 128), F32),
         in_specs=[pl.BlockSpec(memory_space=pltpu.HBM)] * 4,
-        out_specs=[
-            pl.BlockSpec(memory_space=pltpu.HBM),
-            pl.BlockSpec(memory_space=pltpu.VMEM),
-        ],
+        out_specs=pl.BlockSpec(memory_space=pltpu.VMEM),
         scratch_shapes=[
             pltpu.SMEM((blocks,), jnp.int32),
             pltpu.SMEM((NF,), jnp.int32),
@@ -374,6 +391,7 @@
             vm((2, nb // 4, nb * 4), F32),
             vm((2, FCAP, nb // 4, nb * 4), F32),
             vm((size, size), F32),
+            vm((3 * size, size), BF16),
             dma((3,)),
             dma((quarters,)),
             dma((quarters, 3)),
@@ -382,24 +400,21 @@
             dma((2, sps)),
             dma((2, sps)),
             dma((2, FCAP)),
-            *[vm((2, PAIR_CAP, blocks, 2 * QP), F32) for _ in range(quarters)],
+            vm((quarters, 2, PAIR_CAP, blocks, 2 * QP), F32),
+            vm((2, PAIR_CAP, blocks, 2 * QP), F32),
         ],
         compiler_params=pltpu.CompilerParams(
             collective_id=0, has_side_effects=True, vmem_limit_bytes=VMEM_BYTES
         ),
     )(block_starts, owner, table, snapshots)
-    tiles = points // 128
     modes = pl.pallas_call(
-        finish_kernel,
-        grid=(FCAP,),
-        out_shape=jax.ShapeDtypeStruct((size * tiles * 2, 128), F32),
-        in_specs=[
-            pl.BlockSpec((1, nb // 4, nb * 4), lambda s: (s, 0, 0)),
-            pl.BlockSpec((quarters, 2, nb, 2 * QP), lambda s: (0, 0, s, 0)),
-        ],
-        out_specs=pl.BlockSpec((nb * tiles * 2, 128), lambda s: (s, 0)),
+        hand_over,
+        out_shape=jax.ShapeDtypeStruct(modes.shape, F32),
+        in_specs=[pl.BlockSpec(memory_space=pltpu.HBM)],
+        out_specs=pl.BlockSpec(memory_space=pltpu.HBM),
+        scratch_shapes=[dma((2 * FCAP,))],
         compiler_params=pltpu.CompilerParams(vmem_limit_bytes=VMEM_BYTES),
-    )(factors, basis)
+    )(modes)
     modes = modes.reshape(FCAP, nb, tiles, 2, 128).transpose(0, 1, 3, 2, 4)
     return modes.reshape(FCAP, nb, 2, points)
 

time: 46.5 us -> 84.9 us (1.83)
  Pallas kernels: 46.3 us -> 84.7 us
    pallas_call x2, Pallas kernels: 46.3 us -> 84.7 us  [the longest x1 43.8 us: local(): pl.pallas_call(functools.partial(kernel, tms, sps), out_shape=jax.ShapeDt...]
where the time goes in v5:
time: 84.9 us; the launch traced here: 84.8 us
  Pallas kernels  84.7 us (100%)
    pallas_call x1, Pallas kernels, local(): pl.pallas_call(functools.partial(kernel, tms, sps), out_shape=jax.ShapeDt...  43.8 us
    pallas_call x1, Pallas kernels, local(): pl.pallas_call(hand_over, out_shape=jax.ShapeDtypeStruct(modes.shape, F32...  40.9 us

profile of v5, /device:TPU:0, one launch (start us, length us, event | category | flops | bytes accessed | tf_op | source)
XLA Modules:
  0.0 84.8 jit_solution(17153897531090904213)
XLA Ops:
  0.0 43.8 %shard_map.46.source = f32[2560,128]{1,0:T(8,128)} custom-call(s32[8]{0:T(128)} %starts_hbm.1, s32[9]{0:T(128)} %owner_hbm.1, f32[18,256]{1,0:T(8,128)} %constant.2.clone.tab_hbm, f32[1152,1024]{1,0:T(8,128)} %snap_hbm.1), custom_call_target="tpu_custom_call" | custom-call | tf_op jit(solution)/shard_map/pallas_call | solution.py:369
  43.9 40.9 %shard_map.47 = f32[2560,128]{1,0:T(8,128)} custom-call(f32[2560,128]{1,0:T(8,128)} %shard_map.46.source), custom_call_target="tpu_custom_call" | custom-call | tf_op jit(solution)/shard_map/pallas_call | solution.py:410

commit v6 on v2

--- a/solution.py
+++ b/solution.py
@@ -12,6 +12,8 @@
 NF = 9
 FCAP = 5
 PAIR_CAP = 7
+GAP = 112
+VMEM_BYTES = 64 * 1024 * 1024 - 65536
 ROWS = 2 * NF
 QP = 256
 F32 = jnp.float32
@@ -59,13 +61,12 @@
     return jnp.concatenate([packed[:, n * i : n * i + n] for i in range(4)], axis=0)
 
 
-def inverse_factor(gram, panel=8):
+def inverse_factor(gram, empty, panel=8):
     n = gram.shape[0]
     row = lax.broadcasted_iota(jnp.int32, (n, n), 0)
     col = lax.broadcasted_iota(jnp.int32, (n, n), 1)
     eye = jnp.where(row == col, 1.0, 0.0).astype(F32)
-    trace = jnp.sum(jnp.sum(gram * eye, axis=1, keepdims=True), axis=0, keepdims=True)
-    gram = gram + jnp.where(trace == 0.0, 1.0, 0.0) * eye
+    gram = gram + jnp.where(empty, 1.0, 0.0) * eye
     work = jnp.concatenate([eye, gram, jnp.zeros((n, 128 - 2 * n), F32)], axis=1)
     rows = lax.broadcasted_iota(jnp.int32, (n, 128), 0)
     diag = jnp.ones((n, 128), F32)
@@ -78,7 +79,7 @@
             k = first + j
             pivot = jnp.broadcast_to(cols[j][k : k + 1], (n, 128))
             diag = jnp.where(rows == k, pivot, diag)
-            factor = jnp.where(rows > k, cols[j] / pivot, 0.0)
+            factor = jnp.where(rows > k, cols[j] * (1.0 / cols[j][k : k + 1]), 0.0)
             work = work - factor * work[k : k + 1]
             for i in range(j + 1, panel):
                 cols[i] = cols[i] - factor * cols[i][k : k + 1]
@@ -122,12 +123,17 @@
         pl.semaphore_signal(barrier, inc=1, device_id={"tm": peer}, device_id_type=MESH)
     for r in range(1, sps):
         pl.semaphore_signal(barrier, inc=1, device_id={"space": lax.rem(my + r, sps)}, device_id_type=MESH)
+    tallf[...] = jnp.zeros(tallf.shape, F32)
     for load in small:
         load.wait()
 
-    wide = jnp.concatenate([tab_ref[...], jnp.zeros((ROWS, samples - NFFT), F32)], axis=1)
+    span = 2 * NFFT
+    wide = jnp.concatenate([tab_ref[...], jnp.zeros((ROWS, span - NFFT), F32)], axis=1)
     for k in range(blocks):
-        tallf[:, k, :] = pltpu.roll(wide, starts_ref[k] - me * samples, 1)
+        base = k * GAP // 128 * 128
+        keep = min(span, samples - base)
+        moved = pltpu.roll(wide, starts_ref[k] - me * samples - base, 1)
+        tallf[:, k, base : base + keep] = moved[:, :keep]
     tall[...] = jnp.concatenate(split3(tallf[...].reshape(ROWS * blocks, samples)), axis=0)
 
     owners = [owner_ref[f] for f in range(NF)]
@@ -147,7 +153,7 @@
             place = jnp.where(hit, pair_rank[f], place)
         return freq, place
 
-    mine = [owned(me, s) for s in range(FCAP)]
+    held = [owned(me, s) for s in range(FCAP)]
     theirs = [owned(sibling, s)[0] for s in range(FCAP)]
     distant = []
     for place in range(PAIR_CAP):
@@ -187,7 +193,7 @@
             pl.semaphore_wait(barrier, sps + 1)
         across_hops[q].start()
         for s in range(FCAP):
-            near[q, 0, s] = spec[mine[s][0]]
+            near[q, 0, s] = spec[held[s][0]]
             near[q, 1, s] = spec[theirs[s]]
         sibling_hops[q].start()
 
@@ -220,7 +226,11 @@
             total = gbuf[turn, 0]
             for source in range(1, sps):
                 total = total + gbuf[turn, source]
-            inverse = pack(inverse_factor(unpack(total) / rows_total))
+            freq = held[0][0]
+            for s in range(1, FCAP):
+                freq = jnp.where(mine == s, held[s][0], freq)
+            empty = freq == NF
+            inverse = pack(inverse_factor(unpack(total * (1.0 / rows_total)), empty))
             pinv[turn] = inverse
             ibuf[turn, mine] = inverse
             copies = []
@@ -262,7 +272,7 @@
         xbuf[me] = near[q, 0]
         xbuf[sibling] = sib_in[q]
         for s in range(FCAP):
-            freq, place = mine[s]
+            freq, place = held[s]
             xbuf[across, s] = jnp.where(freq < NF, far_in[q][0, place], 0.0)
             xbuf[across_sibling, s] = jnp.where(freq < NF, far_in[q][1, place], 0.0)
         stacked = jnp.concatenate(
@@ -296,16 +306,39 @@
 
     d1, d2 = split2(bd[...])
     d21 = jnp.concatenate([d1, d2], axis=0)
+    tiles = quarters * QP // 128
     for q in range(quarters):
         p1 = mm(d21, bs[q, 0])
         modes = p1[:size] + (p1[size:] + mm(d1, bs[q, 1]))
-        for s in range(FCAP):
-            for c in range(2):
-                part = modes[s * nb : (s + 1) * nb, c * QP : (c + 1) * QP]
-                out_ref[s, :, c, q * QP : (q + 1) * QP] = part
+        for c in range(2):
+            for t in range(QP // 128):
+                at = 2 * (q * (QP // 128) + t) + c
+                lane = c * QP + t * 128
+                out_ref[pl.ds(at, size, stride=2 * tiles), :] = modes[:, lane : lane + 128]
     for q in range(quarters):
         for copy in (across_hops[q], sibling_hops[q], relays[q]):
             copy.wait_send()
+
+
+def hand_over(source, target, held, sem_in, sem_out):
+    chunks = sem_in.shape[0]
+    rows = source.shape[0] // chunks
+    parts = [pl.ds(i * rows, rows) for i in range(chunks)]
+    reads = [
+        pltpu.make_async_copy(source.at[part], held.at[part], sem_in.at[i])
+        for i, part in enumerate(parts)
+    ]
+    writes = [
+        pltpu.make_async_copy(held.at[part], target.at[part], sem_out.at[i])
+        for i, part in enumerate(parts)
+    ]
+    for read in reads:
+        read.start()
+    for read, write in zip(reads, writes):
+        read.wait()
+        write.start()
+    for write in writes:
+        write.wait()
 
 
 def local(tms, sps, snapshots, block_starts, owner):
@@ -314,12 +347,13 @@
     nb = blocks * tms
     size = FCAP * nb
     quarters = points // QP
+    tiles = points // 128
     table = jnp.asarray(dft_table())
     vm = pltpu.VMEM
     dma = pltpu.SemaphoreType.DMA
-    return pl.pallas_call(
+    modes = pl.pallas_call(
         functools.partial(kernel, tms, sps),
-        out_shape=jax.ShapeDtypeStruct((FCAP, nb, 2, points), F32),
+        out_shape=jax.ShapeDtypeStruct((size * tiles * 2, 128), F32),
         in_specs=[pl.BlockSpec(memory_space=pltpu.HBM)] * 4,
         out_specs=pl.BlockSpec(memory_space=pltpu.VMEM),
         scratch_shapes=[
@@ -353,9 +387,19 @@
             *[vm((2, PAIR_CAP, blocks, 2 * QP), F32) for _ in range(quarters)],
         ],
         compiler_params=pltpu.CompilerParams(
-            collective_id=0, has_side_effects=True, vmem_limit_bytes=64 * 1024 * 1024 - 65536
+            collective_id=0, has_side_effects=True, vmem_limit_bytes=VMEM_BYTES
         ),
     )(block_starts, owner, table, snapshots)
+    modes = pl.pallas_call(
+        hand_over,
+        out_shape=jax.ShapeDtypeStruct(modes.shape, F32),
+        in_specs=[pl.BlockSpec(memory_space=pltpu.HBM)],
+        out_specs=pl.BlockSpec(memory_space=pltpu.HBM),
+        scratch_shapes=[vm(modes.shape, F32), dma((FCAP,)), dma((FCAP,))],
+        compiler_params=pltpu.CompilerParams(vmem_limit_bytes=VMEM_BYTES),
+    )(modes)
+    modes = modes.reshape(FCAP, nb, tiles, 2, 128).transpose(0, 1, 3, 2, 4)
+    return modes.reshape(FCAP, nb, 2, points)
 
 
 def solution(mesh):

time: 46.1 us -> 45 us (0.976)
  local copies, waits for them, and re-layouts: 2.86 us -> 0 us
  Pallas kernels: 43.1 us -> 44.8 us
    unnamed x1 -> x0, local copies, waits for them, and re-layouts: 2.86 us -> none
    pallas_call x0 -> x1, Pallas kernels: none -> 2.08 us  [local(): pl.pallas_call(hand_over, out_shape=jax.ShapeDtypeStruct(modes.shape, F32...]
where the time goes in v6:
time: 45 us; the launch traced here: 44.8 us
  Pallas kernels  44.8 us (100%)
    pallas_call x1, Pallas kernels, local(): pl.pallas_call(functools.partial(kernel, tms, sps), out_shape=jax.ShapeDt...  42.7 us
    pallas_call x1, Pallas kernels, local(): pl.pallas_call(hand_over, out_shape=jax.ShapeDtypeStruct(modes.shape, F32...  2.08 us

profile of v6, /device:TPU:0, one launch (start us, length us, event | category | flops | bytes accessed | tf_op | source)
XLA Modules:
  0.0 44.8 jit_solution(1316302568283691985)
XLA Ops:
  0.0 42.7 %shard_map.46.source = f32[2560,128]{1,0:T(8,128)} custom-call(s32[8]{0:T(128)} %starts_hbm.1, s32[9]{0:T(128)} %owner_hbm.1, f32[18,256]{1,0:T(8,128)} %constant.2.clone.tab_hbm, f32[1152,1024]{1,0:T(8,128)} %snap_hbm.1), custom_call_target="tpu_custom_call" | custom-call | tf_op jit(solution)/shard_map/pallas_call | solution.py:354
  42.7 2.1 %shard_map.47 = f32[2560,128]{1,0:T(8,128)} custom-call(f32[2560,128]{1,0:T(8,128)} %shard_map.46.source), custom_call_target="tpu_custom_call" | custom-call | tf_op jit(solution)/shard_map/pallas_call | solution.py:393

commit v7 on v6

--- a/solution.py
+++ b/solution.py
@@ -68,22 +68,25 @@
     eye = jnp.where(row == col, 1.0, 0.0).astype(F32)
     gram = gram + jnp.where(empty, 1.0, 0.0) * eye
     work = jnp.concatenate([eye, gram, jnp.zeros((n, 128 - 2 * n), F32)], axis=1)
-    rows = lax.broadcasted_iota(jnp.int32, (n, 128), 0)
-    diag = jnp.ones((n, 128), F32)
+    done = []
     for first in range(0, n, panel):
+        left = n - first
+        rows = lax.broadcasted_iota(jnp.int32, (left, 128), 0)
+        diag = jnp.ones((panel, 128), F32)
         cols = [
-            jnp.broadcast_to(work[:, n + first + j : n + first + j + 1], (n, 128))
+            jnp.broadcast_to(work[:, n + first + j : n + first + j + 1], (left, 128))
             for j in range(panel)
         ]
         for j in range(panel):
-            k = first + j
-            pivot = jnp.broadcast_to(cols[j][k : k + 1], (n, 128))
-            diag = jnp.where(rows == k, pivot, diag)
-            factor = jnp.where(rows > k, cols[j] * (1.0 / cols[j][k : k + 1]), 0.0)
-            work = work - factor * work[k : k + 1]
+            pivot = cols[j][j : j + 1]
+            diag = jnp.where(rows[:panel] == j, pivot, diag)
+            factor = jnp.where(rows > j, cols[j] * (1.0 / pivot), 0.0)
+            work = work - factor * work[j : j + 1]
             for i in range(j + 1, panel):
-                cols[i] = cols[i] - factor * cols[i][k : k + 1]
-    return (work / jnp.sqrt(diag))[:, :n]
+                cols[i] = cols[i] - factor * cols[i][j : j + 1]
+        done.append(work[:panel] / jnp.sqrt(diag))
+        work = work[panel:]
+    return jnp.concatenate(done, axis=0)[:, :n]
 
 
 def kernel(

time: 45 us -> 45 us (level)
  no operation moved by 1% of the time
where the time goes in v7:
time: 45 us; the launch traced here: 44.8 us
  Pallas kernels  44.8 us (100%)
    pallas_call x1, Pallas kernels, local(): pl.pallas_call(functools.partial(kernel, tms, sps), out_shape=jax.ShapeDt...  42.7 us
    pallas_call x1, Pallas kernels, local(): pl.pallas_call(hand_over, out_shape=jax.ShapeDtypeStruct(modes.shape, F32...  2.08 us

profile of v7, /device:TPU:0, one launch (start us, length us, event | category | flops | bytes accessed | tf_op | source)
XLA Modules:
  0.0 44.8 jit_solution(3002749051496745256)
XLA Ops:
  0.0 42.7 %shard_map.46.source = f32[2560,128]{1,0:T(8,128)} custom-call(s32[8]{0:T(128)} %starts_hbm.1, s32[9]{0:T(128)} %owner_hbm.1, f32[18,256]{1,0:T(8,128)} %constant.2.clone.tab_hbm, f32[1152,1024]{1,0:T(8,128)} %snap_hbm.1), custom_call_target="tpu_custom_call" | custom-call | tf_op jit(solution)/shard_map/pallas_call | solution.py:357
  42.7 2.1 %shard_map.47 = f32[2560,128]{1,0:T(8,128)} custom-call(f32[2560,128]{1,0:T(8,128)} %shard_map.46.source), custom_call_target="tpu_custom_call" | custom-call | tf_op jit(solution)/shard_map/pallas_call | solution.py:396
